TPU v7x, 128 devices: a whole 4x4x4 slice. The times are simulated.
128 devices in a mesh: row: 16 (over z, y_hi, core), col: 8 (over y_lo, x).
Axes of the slice: x: 4, y: 4 (y_hi: 2, y_lo: 2; y = y_hi * 2 + y_lo), z: 4, core: 2. Of those that a mesh axis runs over, the one named last changes fastest.
Arguments:
- nodes: bfloat16 [32768, 512], P(('row', 'col')), may hold values from -6 to 6
- gain: float32 [512], replicated, may hold values from 0.1 to 1.9
- w_query: bfloat16 [512, 512], replicated
- w_key: bfloat16 [512, 512], replicated
- w_value: bfloat16 [512, 512], replicated, may hold values from -0.25 to 0.25
- w_out: bfloat16 [512, 512], replicated, may hold values from -0.75 to 0.75
- cotangent: bfloat16 [32768, 512], P(('row', 'col')), may hold values from -6 to 6
- tile_index: int32 [16, 8, 32, 2], P('row', 'col'), may hold values from 0 to 31, as said below
- tile_mask: int32 [16, 8, 32, 128, 128], P('row', 'col'), may hold values from 0 to 1, as said below
- tile_count: int32 [16, 8], P('row', 'col'), may hold values from 4 to 32, as said below
- node_order: int32 [32768], P(('row', 'col')), may hold values from 0 to 32767, as said below
Outputs:
- update: bfloat16 [32768, 512], P(('row', 'col'))
- node_grad: bfloat16 [32768, 512], P(('row', 'col'))
Inputs may be any that keep to these rules, and one draw needn't show every extreme that they name: tile_index[i, j, t] = (r, s): r below 16, s below 32; the pairs of one cell are distinct; for t < 2 the pair is (j * 2 + t, i * 2 + t). `tile_mask`: the first 2 slots of every cell hold 1 on the diagonal. Slots of a cell at or after its tile_count are unused and hold arbitrary pairs and masks. `node_order`: a permutation of the 32768 nodes; the 256 owner rows of device p = i * 8 + j hold the nodes p * 256 to (p + 1) * 256 - 1 in some order.
All inputs are finite; a program needn't handle non-finite values.
Results may differ from a plain program's by a relative error of at most 0.022.
Values may be sent and summed in bfloat16 or wider, within the bound.
A program may use at most 128 MiB of HBM per device.

v0:
```python
import jax
import jax.numpy as jnp
from jax import lax
from jax.sharding import PartitionSpec as P

HEADS = 4


epsilon = 1e-05
tiles_per_step = 8


def normalize(node_rows):
    values_f = node_rows.astype(jnp.float32)
    center = values_f - jnp.mean(values_f, axis=1, keepdims=True)
    inv_std = lax.rsqrt(jnp.mean(center * center, axis=1, keepdims=True) + epsilon)
    return (center * inv_std, inv_std)


def group_scores(query_tile, key_tile, edge_mask, score_scale):
    scores = (
        jnp.einsum("gahd,gbhd->ghab", query_tile, key_tile, preferred_element_type=jnp.float32)
        * score_scale
    )
    return jnp.where(edge_mask[:, None], scores, -jnp.inf)


def exact_back(grads, weight):
    return jnp.dot(grads, weight.astype(jnp.float32).T, precision=lax.Precision.HIGHEST)


def local(
    nodes,
    gain,
    w_query,
    w_key,
    w_value,
    w_out,
    cotangent,
    tile_index,
    tile_mask,
    tile_count,
    node_order,
):
    own_rows, model_width = nodes.shape
    head_count = HEADS
    head_dim = model_width // head_count
    tile_side = tile_mask.shape[-1]
    slot_count = tile_mask.shape[2]
    score_scale = head_dim ** (-0.5)
    local_slot = node_order % own_rows
    graph_nodes = jnp.zeros_like(nodes).at[local_slot].set(nodes)
    unit_rows, inv_std = normalize(graph_nodes)
    normed = (unit_rows * gain).astype(jnp.bfloat16)
    query = jnp.dot(normed, w_query, preferred_element_type=jnp.float32).astype(jnp.bfloat16)
    joint_w = jnp.concatenate((w_key, w_value), axis=1)
    own_pair = jnp.dot(normed, joint_w, preferred_element_type=jnp.float32).astype(jnp.bfloat16)
    pair_rows = lax.all_gather(own_pair, "row", axis=0, tiled=True)
    query_recv = lax.all_gather(query, "col", axis=0, tiled=True)
    recv_blocks = query_recv.shape[0] // tile_side
    send_blocks = pair_rows.shape[0] // tile_side
    query_blocks = query_recv.reshape(recv_blocks, tile_side, head_count, head_dim)
    pair_blocks = pair_rows.reshape(send_blocks, tile_side, 2 * head_count, head_dim)
    recv_all = tile_index[0, 0, :, 0]
    send_all = tile_index[0, 0, :, 1]
    live_slot = jnp.arange(slot_count, dtype=jnp.int32) < tile_count[0, 0]
    edge_all = (tile_mask[0, 0] > 0) & live_slot[:, None, None]
    loop_turns = slot_count // tiles_per_step

    def group_tiles(turn_id):
        first_slot = turn_id * tiles_per_step
        recv_idx = lax.dynamic_slice_in_dim(recv_all, first_slot, tiles_per_step, 0)
        send_idx = lax.dynamic_slice_in_dim(send_all, first_slot, tiles_per_step, 0)
        edge_mask = lax.dynamic_slice_in_dim(edge_all, first_slot, tiles_per_step, 0)
        query_tile = query_blocks[recv_idx]
        pair_tile = pair_blocks[send_idx]
        key_tile = pair_tile[:, :, :head_count]
        value_tile = pair_tile[:, :, head_count:]
        scores = group_scores(query_tile, key_tile, edge_mask, score_scale)
        return (recv_idx, send_idx, query_tile, key_tile, value_tile, scores)

    def max_step(turn_id, row_top):
        recv_idx, send_idx, query_tile, key_tile, value_tile, scores = group_tiles(turn_id)
        return row_top.at[recv_idx].max(jnp.max(scores, axis=3))

    start_top = jnp.full((recv_blocks, head_count, tile_side), -jnp.inf, jnp.float32)
    local_top = lax.fori_loop(0, loop_turns, max_step, start_top)
    row_top = lax.pmax(local_top, "col")

    def sum_step(turn_id, carried):
        weighted, totals = carried
        recv_idx, send_idx, query_tile, key_tile, value_tile, scores = group_tiles(turn_id)
        weight = jnp.exp(scores - row_top[recv_idx][..., None])
        totals = totals.at[recv_idx].add(jnp.sum(weight, axis=3))
        weighted = weighted.at[recv_idx].add(
            jnp.einsum(
                "ghab,gbhd->gahd",
                weight.astype(jnp.bfloat16),
                value_tile,
                preferred_element_type=jnp.float32,
            )
        )
        return (weighted, totals)

    zero_recv = jnp.zeros((recv_blocks, tile_side, head_count, head_dim), jnp.float32)
    zero_totals = jnp.zeros((recv_blocks, head_count, tile_side), jnp.float32)
    weighted, totals = lax.fori_loop(0, loop_turns, sum_step, (zero_recv, zero_totals))
    own_start = lax.axis_index("col") * own_rows
    weighted_all, totals_all = (
        lax.psum(weighted.astype(jnp.bfloat16), "col").astype(jnp.float32),
        lax.psum(totals.astype(jnp.bfloat16), "col").astype(jnp.float32),
    )
    attended_all = (
        (weighted_all / totals_all.transpose(0, 2, 1)[..., None])
        .reshape(-1, model_width)
        .astype(jnp.bfloat16)
    )
    attended = lax.dynamic_slice_in_dim(attended_all, own_start, own_rows, 0)
    update = jnp.dot(attended, w_out, preferred_element_type=jnp.float32).astype(jnp.bfloat16)
    graph_grad = jnp.zeros_like(cotangent).at[local_slot].set(cotangent)
    d_attn = lax.dot_general(
        graph_grad, w_out, (((1,), (1,)), ((), ())), preferred_element_type=jnp.float32
    ).astype(jnp.bfloat16)
    grad_recv = lax.all_gather(d_attn, "col", axis=0, tiled=True)
    product = grad_recv.astype(jnp.float32) * attended_all.astype(jnp.float32)
    row_deltas = jnp.sum(
        product.reshape(recv_blocks, tile_side, head_count, head_dim), axis=3
    ).transpose(0, 2, 1)
    grad_blocks = grad_recv.reshape(recv_blocks, tile_side, head_count, head_dim)

    def grad_step(turn_id, carried):
        query_acc, key_acc, value_acc = carried
        recv_idx, send_idx, query_tile, key_tile, value_tile, scores = group_tiles(turn_id)
        grad_tile = grad_blocks[recv_idx]
        norm_weight = (
            jnp.exp(scores - row_top[recv_idx][..., None]) / totals_all[recv_idx][..., None]
        )
        d_prob = jnp.einsum(
            "gahd,gbhd->ghab", grad_tile, value_tile, preferred_element_type=jnp.float32
        )
        d_score = (norm_weight * (d_prob - row_deltas[recv_idx][..., None]) * score_scale).astype(
            jnp.bfloat16
        )
        query_acc = query_acc.at[recv_idx].add(
            jnp.einsum("ghab,gbhd->gahd", d_score, key_tile, preferred_element_type=jnp.float32)
        )
        key_acc = key_acc.at[send_idx].add(
            jnp.einsum("ghab,gahd->gbhd", d_score, query_tile, preferred_element_type=jnp.float32)
        )
        value_acc = value_acc.at[send_idx].add(
            jnp.einsum(
                "ghab,gahd->gbhd",
                norm_weight.astype(jnp.bfloat16),
                grad_tile,
                preferred_element_type=jnp.float32,
            )
        )
        return (query_acc, key_acc, value_acc)

    zero_send = jnp.zeros((send_blocks, tile_side, head_count, head_dim), jnp.float32)
    query_acc, key_acc, value_acc = lax.fori_loop(
        0, loop_turns, grad_step, (zero_recv, zero_send, zero_send)
    )
    query_grad = lax.psum_scatter(
        query_acc.reshape(-1, model_width).astype(jnp.bfloat16),
        "col",
        scatter_dimension=0,
        tiled=True,
    ).astype(jnp.float32)
    key_flat = key_acc.reshape(-1, model_width)
    value_flat = value_acc.reshape(-1, model_width)
    key_grad, value_grad = (
        lax.psum_scatter(
            key_flat.astype(jnp.bfloat16), "row", scatter_dimension=0, tiled=True
        ).astype(jnp.float32),
        lax.psum_scatter(
            value_flat.astype(jnp.bfloat16), "row", scatter_dimension=0, tiled=True
        ).astype(jnp.float32),
    )
    pair_back = exact_back(key_grad, w_key) + exact_back(value_grad, w_value)
    d_normed = exact_back(query_grad, w_query) + pair_back
    scaled = d_normed * gain
    grad_graph = inv_std * (
        scaled
        - jnp.mean(scaled, axis=1, keepdims=True)
        - unit_rows * jnp.mean(scaled * unit_rows, axis=1, keepdims=True)
    )
    return (update[local_slot], grad_graph.astype(jnp.bfloat16)[local_slot])


def solution(mesh):
    placed = (
        P(("row", "col"), None),
        P(),
        P(),
        P(),
        P(),
        P(),
        P(("row", "col"), None),
        P("row", "col", None, None),
        P("row", "col", None, None, None),
        P("row", "col"),
        P(("row", "col")),
    )
    return jax.shard_map(
        local,
        mesh=mesh,
        in_specs=placed,
        out_specs=(P(("row", "col"), None), P(("row", "col"), None)),
        check_vma=False,
    )
```

profile of v0, /device:TPU:0, one launch (start us, length us, event | category | flops | bytes accessed | tf_op | source)
XLA Modules:
  0.0 849.5 jit_solution(3416196054170434496)
XLA Ops:
  20.4 36.0 %all-gather.6.cloned.1.call-done = bf16[2048,512]{1,0:T(8,128)(2,1)} async-done(((bf16[256,512]{1,0:T(8,128)(2,1)}), bf16[2048,512]{1,0:T(8,128)(2,1)}) %all-gather.6.cloned.1.call-update) | async-done | bytes 2097168 | tf_op jit(solution)/shard_map/all_gather | solution.py:59
  56.4 4.0 reshape.60
  60.4 71.1 %all-gather.4.cloned.1.call-done = bf16[4096,1024]{1,0:T(8,128)(2,1)} async-done(((bf16[256,1024]{1,0:T(8,128)(2,1)}), bf16[4096,1024]{1,0:T(8,128)(2,1)}) %all-gather.4.cloned.1.call-update) | async-done | bytes 8388624 | tf_op jit(solution)/shard_map/all_gather | solution.py:58
  131.5 8.9 %copy.83 = bf16[512,8,8,128]{3,2,1,0:T(8,128)(2,1)} copy(bf16[512,8,8,128]{3,1,2,0:T(8,128)(2,1)} %bitcast.98) | data formatting | bytes 16777216
  140.5 45.4 %while.45 = (s32[]{:T(128)}, f32[16,4,128]{2,1,0:T(4,128)S(1)}, s32[32]{0:T(128)S(1)}, pred[32,128,128]{1,2,0:T(8,128)(4,1)S(1)}, bf16[16,128,4,128]{3,2,1,0:T(4...) while((s32[]{:T(128)}, f32[16,4,128]{2,1,0:T(4,128)S(1)}, ...), condition=%wide.region_6.7_spmd, body=%wide.region_3.6_spmd.sunk | while | flops 135792688 | bytes 15147487 | solution.py:87
  140.6 3.9 gather_fusion.1
  144.5 4.4 gather_fusion
  151.9 4.0 gather_fusion.1
  155.9 4.4 gather_fusion
  163.3 3.9 gather_fusion.1
  167.3 4.4 gather_fusion
  174.7 3.9 gather_fusion.1
  178.6 4.4 gather_fusion
  185.9 33.5 %pmax.7 = f32[16,4,128]{2,1,0:T(4,128)S(1)} all-reduce(f32[16,4,128]{2,1,0:T(4,128)S(1)} %get-tuple-element.497), channel_id=1, replica_groups=mesh['row'=16,'col'=8] {'col'}, use_global_device_ids=true, to_apply=%region_7.8 | all-reduce | flops 8192 | bytes 65536 | tf_op jit(solution)/shard_map/pmax | solution.py:88
  221.9 80.6 %while.46 = (s32[]{:T(128)}, f32[16,128,4,128]{3,1,2,0:T(8,128)}, f32[16,4,128]{2,1,0:T(4,128)S(1)}, s32[32]{0:T(128)S(1)}, s32[32]{0:T(128)S(1)}, /*index=5*/bf...) while((s32[]{:T(128)}, f32[16,128,4,128]{3,1,2,0:T(8,128)}, ...), condition=%wide.region_12.13_spmd, body=%wide.region_8.12_spmd.sunk | while | flops 271583296 | bytes 33022512 | solution.py:107
  222.6 3.9 gather_fusion.4
  226.6 4.4 gather_fusion.2
  237.8 4.3 scatter_fusion.1
  242.8 3.9 gather_fusion.4
  246.7 4.4 gather_fusion.2
  257.9 4.2 scatter_fusion.1
  262.9 3.9 gather_fusion.4
  266.8 4.4 gather_fusion.2
  278.0 4.3 scatter_fusion.1
  283.0 3.9 gather_fusion.4
  286.9 4.4 gather_fusion.2
  298.2 4.3 scatter_fusion.1
  302.5 4.0 convert_element_type.94
  306.6 4.0 reshape.61
  310.6 30.9 %psum.15 = bf16[16,4,128]{2,1,0:T(4,128)(2,1)S(1)} all-reduce(bf16[16,4,128]{2,1,0:T(4,128)(2,1)S(1)} %convert_element_type.96), channel_id=1, replica_groups=mesh['row'=16,'col'=8] {'col'}, use_global_device_ids=true, to_apply=%region_14.15 | all-reduce | flops 8192 | bytes 32768 | tf_op jit(solution)/shard_map/psum | solution.py:111
  341.4 43.2 %all-reduce.2.cloned.1.call-done = bf16[16,128,4,128]{3,1,2,0:T(8,128)(2,1)} async-done(((bf16[16,128,4,128]{3,1,2,0:T(8,128)(2,1)}), bf16[16,128,4,128]{3,1,2,0:T(8,128)(2,1)}) %all-reduce.2.cloned.1.call-update) | async-done | bytes 2097168 | tf_op jit(solution)/shard_map/psum | solution.py:110
  392.9 5.2 reshape.62
  398.1 4.5 reduce_sum.60
  405.5 4.3 broadcast_in_dim.168.clone
  409.7 4.4 broadcast_in_dim.168
  414.1 203.6 %while.47 = (s32[]{:T(128)}, f32[16,128,4,128]{3,1,2,0:T(8,128)}, f32[32,128,4,128]{3,1,2,0:T(8,128)}, f32[32,128,4,128]{3,1,2,0:T(8,128)}, s32[32]{0:T(128)S(1)...) while((s32[]{:T(128)}, f32[16,128,4,128]{3,1,2,0:T(8,128)}, ...), condition=%wide.region_21.22_spmd, body=%wide.region_17.21_spmd.sunk | while | flops 677382208 | bytes 97018680 | solution.py:161
  425.4 5.6 gather_fusion.8
  431.0 3.4 fusion.93
  451.7 4.3 scatter_fusion.3
  456.0 5.0 scatter_fusion.4
  461.1 4.2 scatter_fusion.5
  476.1 5.6 gather_fusion.8
  481.7 3.4 fusion.93
  502.5 4.2 scatter_fusion.3
  506.7 5.0 scatter_fusion.4
  511.7 4.2 scatter_fusion.5
  526.7 5.6 gather_fusion.8
  532.4 3.4 fusion.93
  553.1 4.3 scatter_fusion.3
  557.4 5.1 scatter_fusion.4
  562.5 4.3 scatter_fusion.5
  577.6 5.6 gather_fusion.8
  604.0 4.2 scatter_fusion.3
  608.2 5.2 scatter_fusion.4
  613.4 4.3 scatter_fusion.5
  623.2 3.5 copy.116
  626.8 6.3 convert_element_type.106
  633.2 8.2 copy.74
  641.3 8.3 copy.115
  649.7 6.4 convert_element_type.108
  656.1 7.9 copy.75
  664.0 8.4 copy.114
  677.9 76.9 %reduce-scatter.6.cloned.1.call-done = bf16[256,512]{0,1:T(8,128)(2,1)} async-done(((bf16[4096,512]{0,1:T(8,128)(2,1)}), bf16[256,512]{0,1:T(8,128)(2,1)}) %reduce-scatter.6.cloned.1.call-update) | async-done | bytes 262160 | tf_op jit(solution)/shard_map/reduce_scatter | solution.py:173
  756.2 82.7 %reduce-scatter.8.cloned.1.call-done = bf16[256,512]{0,1:T(8,128)(2,1)} async-done(((bf16[4096,512]{0,1:T(8,128)(2,1)}), bf16[256,512]{0,1:T(8,128)(2,1)}) %reduce-scatter.8.cloned.1.call-update) | async-done | bytes 262160 | tf_op jit(solution)/shard_map/reduce_scatter | solution.py:176
  (293 shorter events, 199.6 us)
Async XLA Ops:
  7.2 10.1 %copy-start = (bf16[512,512]{1,0:T(8,128)(2,1)S(1)}, bf16[512,512]{1,0:T(8,128)(2,1)}, u32[]{:S(2)}) copy-start(bf16[512,512]{1,0:T(8,128)(2,1)} %param.22) | copy-start | bytes 1572868
  7.2 5.4 copy-start.24
  7.2 49.2 %all-gather.6.cloned.1.call-start = ((), (), s32[]{:S(2)}) async-start(), calls=%async_computation.4 | async-start | bytes 2359296 | tf_op jit(solution)/shard_map/all_gather | solution.py:59
  8.0 7.3 copy-start.22
  10.0 5.2 copy-start.11
  10.1 5.1 copy-start.18
  10.3 4.9 copy-start.20
  12.5 6.6 copy-start.26
  12.5 6.6 copy-start.14
  12.5 119.0 %all-gather.4.cloned.1.call-start = ((), (), s32[]{:S(2)}) async-start(), calls=%async_computation.3 | async-start | bytes 8912896 | tf_op jit(solution)/shard_map/all_gather | solution.py:58
  15.2 291.4 %all-gather.8.cloned.1.call-start = ((), (), s32[]{:S(2)}) async-start(), calls=%async_computation.6 | async-start | bytes 2359296 | tf_op jit(solution)/shard_map/all_gather | solution.py:124
  18.3 366.3 %all-reduce.2.cloned.1.call-start = ((), (), s32[]{:S(2)}) async-start(), calls=%async_computation.5 | async-start | bytes 4194304 | tf_op jit(solution)/shard_map/psum | solution.py:110
  19.4 41.0 %copy-start.13 = (pred[32,128,128]{2,1,0:T(8,128)(4,1)}, pred[32,128,128]{2,1,0:T(8,128)(4,1)S(1)}, u32[]{:S(2)}) copy-start(pred[32,128,128]{2,1,0:T(8,128)(4,1)S(1)} %bitcast_and_fusion) | copy-start | bytes 1572868
  148.9 1.2 copy-start.7
  160.3 1.2 copy-start.7
  171.6 1.2 copy-start.7
  183.0 1.2 copy-start.7
  230.9 1.2 copy-start.6
  251.1 1.2 copy-start.6
  271.2 1.2 copy-start.6
  291.3 1.2 copy-start.6
  306.5 370.1 %reduce-scatter.4.cloned.1.call-start = ((), (), s32[]{:S(2)}) async-start(), calls=%async_computation.7 | async-start | bytes 2359296 | tf_op jit(solution)/shard_map/reduce_scatter | solution.py:164
  387.1 3.2 copy-start.10
  388.9 1.4 copy-start.8
  431.0 3.4 copy-start.2
  434.4 2.4 copy-start.4
  439.8 3.0 copy-start.3
  442.9 1.8 copy-start.5
  456.0 5.0 copy-start.1
  481.7 3.4 copy-start.2
  485.1 2.4 copy-start.4
  490.6 3.0 copy-start.3
  493.6 1.8 copy-start.5
  506.7 5.0 copy-start.1
  532.3 3.4 copy-start.2
  535.8 2.4 copy-start.4
  541.2 3.0 copy-start.3
  544.2 1.8 copy-start.5
  557.4 5.1 copy-start.1
  583.3 3.4 copy-start.2
  586.7 2.4 copy-start.4
  592.1 3.0 copy-start.3
  595.1 1.8 copy-start.5
  608.2 5.2 copy-start.1
  626.8 128.1 %reduce-scatter.6.cloned.1.call-start = ((), (), s32[]{:S(2)}) async-start(), calls=%async_computation.8 | async-start | bytes 4456448 | tf_op jit(solution)/shard_map/reduce_scatter | solution.py:173
  649.7 189.3 %reduce-scatter.8.cloned.1.call-start = ((), (), s32[]{:S(2)}) async-start(), calls=%async_computation.9 | async-start | bytes 4456448 | tf_op jit(solution)/shard_map/reduce_scatter | solution.py:176
  672.4 0.7 copy-start.23
  672.4 1.6 copy-start.9
  674.4 2.2 copy-start.15
  674.7 80.2 %copy-start.16 = (bf16[512,512]{1,0:T(8,128)(2,1)S(1)}, bf16[512,512]{1,0:T(8,128)(2,1)}, u32[]{:S(2)}) copy-start(bf16[512,512]{1,0:T(8,128)(2,1)} %param.20) | copy-start | bytes 1572868
  674.7 164.2 %copy-start.12 = (bf16[256,512]{1,0:T(8,128)(2,1)S(1)}, bf16[256,512]{1,0:T(8,128)(2,1)}, u32[]{:S(2)}) copy-start(bf16[256,512]{1,0:T(8,128)(2,1)} %copy-done.11) | copy-start | bytes 786436
  674.7 164.2 %copy-start.17 = (bf16[512,512]{1,0:T(8,128)(2,1)S(1)}, bf16[512,512]{1,0:T(8,128)(2,1)}, u32[]{:S(2)}) copy-start(bf16[512,512]{1,0:T(8,128)(2,1)} %param.21) | copy-start | bytes 1572868
  674.7 164.2 %copy-start.19 = (f32[256]{0:T(256)S(1)}, f32[256]{0:T(256)}, u32[]{:S(2)}) copy-start(f32[256]{0:T(256)} %copy-done.18) | copy-start | bytes 3076
  674.7 164.2 %copy-start.21 = (f32[256]{0:T(256)S(1)}, f32[256]{0:T(256)}, u32[]{:S(2)}) copy-start(f32[256]{0:T(256)} %copy-done.20) | copy-start | bytes 3076
  674.8 164.2 %copy-start.25 = (f32[512]{0:T(512)S(1)}, f32[512]{0:T(512)}, u32[]{:S(2)}) copy-start(f32[512]{0:T(512)} %param.18) | copy-start | bytes 6148
Sparse Core Ops, SparseCore 0:
  12.6 43.7 all-gather.5
  58.9 72.5 all-gather.3
  133.7 38.9 all-gather.7
  306.6 77.9 all-reduce.1
  626.9 44.6 reduce-scatter.3
  675.4 79.3 reduce-scatter.5
  759.4 79.4 reduce-scatter.7
where the time goes:
time: 860 us; the launch traced here: 850 us
  waiting for transfers between devices  310 us (36%)
  local copies, waits for them, and re-layouts  286 us (33%)
  other arithmetic  109 us (13%)
  blocking collectives  64.4 us (7%)
  matrix products  62.8 us (7%)
  between operations  15.3 us (2%)
    reduce_scatter x1, waiting for transfers between devices, local(): lax.psum_scatter(value_flat.astype(jnp.bfloat16), 'row', scatter_dimensio...  82.7 us
    reduce_scatter x1, waiting for transfers between devices, local(): lax.psum_scatter(key_flat.astype(jnp.bfloat16), 'row', scatter_dimension=...  76.9 us
    all_gather x1, waiting for transfers between devices, local(): pair_rows = lax.all_gather(own_pair, 'row', axis=0, tiled=True)  71.1 us
    gather x12, local copies, waits for them, and re-layouts, group_tiles(): pair_tile = pair_blocks[send_idx]  57.6 us
    gather x16, local copies, waits for them, and re-layouts, group_tiles(): query_tile = query_blocks[recv_idx]  48.9 us
    psum x1, waiting for transfers between devices, local(): lax.psum(weighted.astype(jnp.bfloat16), 'col').astype(jnp.float32)  43.2 us
    all_gather x1, waiting for transfers between devices, local(): query_recv = lax.all_gather(query, 'col', axis=0, tiled=True)  36 us
    pmax x1, blocking collectives, local(): row_top = lax.pmax(local_top, 'col')  33.5 us
  transfers between devices with their start and end apart: 7, of which 5 were waited for; matrix products, arithmetic and copies ran while one was open for 24% of the time, Pallas kernels for 0%

commit v1 on v0

v1 whole, which is shorter than its diff:
```python
import jax
import jax.numpy as jnp
from jax import lax
from jax.experimental import pallas as pl
from jax.experimental.pallas import tpu as pltpu
from jax.sharding import PartitionSpec as P

HEADS = 4
HD = 128
D = 512
TB = 128
OWN = 256
TILES = 32
RB = 16
SB = 32
EPS = 1e-05
LOG2E = 1.4426950408889634
SCALE = HD ** (-0.5)
FLOOR = -3.4028235e38
MESH = pl.DeviceIdType.MESH
F32 = jnp.float32
BF16 = jnp.bfloat16
SEMS = 256
UNROLL = 4


def mm(a, b):
    return jnp.dot(a, b, preferred_element_type=F32)


def mm_nt(a, b):
    return lax.dot_general(a, b, (((1,), (1,)), ((), ())), preferred_element_type=F32)


def mm_tn(a, b):
    return lax.dot_general(a, b, (((0,), (0,)), ((), ())), preferred_element_type=F32)


def body(
    meta,
    order,
    rcol,
    nodes,
    cot,
    gain,
    wq,
    wk,
    wv,
    wo,
    mask,
    out_update,
    out_grad,
    perm_s,
    unit_s,
    inv_s,
    nall,
    qd0,
    qd1,
    qd2,
    qd3,
    kv,
    bias,
    wgt,
    dpr,
    m_s,
    l_s,
    d_s,
    p_s,
    ds_s,
    acc1,
    acc2,
    od,
    ra,
    rb,
    rd,
    fin,
    dkv,
    pd,
    pa,
    pb,
    pe,
    st_send,
    st_recv,
    gs0,
    gs1,
    gs2,
    gs3,
    ss,
    rs,
):
    qd = [qd0, qd1, qd2, qd3]
    gstat = [gs0, gs1, gs2, gs3]
    i = lax.axis_index("row")
    j = lax.axis_index("col")
    z, yh, c = i // 4, (i // 2) % 2, i % 2
    yl, x = j // 4, j % 4

    def row_id(z_, yh_, c_):
        return (z_ * 2 + yh_) * 2 + c_

    def col_id(yl_, x_):
        return yl_ * 4 + x_

    zp, zm, zo = (z + 1) % 4, (z + 3) % 4, (z + 2) % 4
    xp, xm, xo = (x + 1) % 4, (x + 3) % 4, (x + 2) % 4
    oh, ol, oc = 1 - yh, 1 - yl, 1 - c
    sib = (row_id(z, yh, oc), j)
    yhp = (row_id(z, oh, c), j)
    dzp = (row_id(zp, yh, c), j)
    dzm = (row_id(zm, yh, c), j)
    ylp = (i, col_id(ol, x))
    dxp = (i, col_id(yl, xp))
    dxm = (i, col_id(yl, xm))

    made = []

    def copy(src, dst, dev):
        k = len(made)
        d = pltpu.make_async_remote_copy(
            src_ref=src,
            dst_ref=dst,
            send_sem=ss.at[k],
            recv_sem=rs.at[k],
            device_id=dev,
            device_id_type=MESH,
        )
        made.append(d)
        d.start()
        return d

    peers = [(i, lax.rem(j + k, 8)) for k in range(1, 8)]
    barrier = pltpu.get_barrier_semaphore()
    for dev in [sib, yhp, dzp, dzm] + peers:
        pl.semaphore_signal(barrier, inc=1, device_id=dev, device_id_type=MESH)

    perm = jnp.where(
        lax.broadcasted_iota(jnp.int32, (OWN, OWN), 0) == order[...], 1.0, 0.0
    ).astype(BF16)
    perm_s[...] = perm
    rows = mm(perm, nodes[...])
    center = rows - jnp.mean(rows, axis=1, keepdims=True)
    inv = lax.rsqrt(jnp.mean(center * center, axis=1, keepdims=True) + EPS)
    unit = center * inv
    unit_s[...] = unit
    inv_s[...] = jnp.broadcast_to(inv, (OWN, 128))
    normed = (unit * gain[...]).astype(BF16)
    own = row_id(z, yh, c)
    nall[own] = normed
    query = mm(normed, wq[...]).astype(BF16)
    grads = mm_nt(mm(perm, cot[...]).astype(BF16), wo[...]).astype(BF16)
    for h in range(HEADS):
        cols = slice(h * HD, (h + 1) * HD)
        for a in range(2):
            qd[h][2 * j + a, 0] = query[a * TB : (a + 1) * TB, cols]
            qd[h][2 * j + a, 1] = grads[a * TB : (a + 1) * TB, cols]

    pl.semaphore_wait(barrier, 11)

    def nsend(b, dev):
        return copy(nall.at[b], nall.at[b], dev)

    def nhalf(b, half, dev):
        part = nall.at[b, pl.ds(half * TB, TB)]
        return copy(part, part, dev)

    def qsend(h, b, dev):
        part = qd[h].at[pl.ds(2 * b, 2)]
        return copy(part, part, dev)

    def qhalf(h, b, half, dev):
        part = qd[h].at[2 * b + half]
        return copy(part, part, dev)

    n_y = nsend(own, yhp)
    n_p = nsend(own, dzp)
    n_m = nsend(own, dzm)
    sibs = [nsend(own, sib)]
    cy, cp, cm = [], [], []
    for h in range(HEADS):
        cy.append(qsend(h, j, ylp))
        cp.append(qsend(h, j, dxp))
        cm.append(qsend(h, j, dxm))

    def project(b):
        rows = nall[b]
        k_rows = mm(rows, wk[...]).astype(BF16)
        v_rows = mm(rows, wv[...]).astype(BF16)
        for h in range(HEADS):
            cols = slice(h * HD, (h + 1) * HD)
            for a in range(2):
                kv[h, 2 * b + a, 0] = k_rows[a * TB : (a + 1) * TB, cols]
                kv[h, 2 * b + a, 1] = v_rows[a * TB : (a + 1) * TB, cols]

    def make_bias(t, carry):
        tile = mask[meta[2, t]].astype(F32)
        bias[t] = jnp.where(tile.T > meta[4, t].astype(F32), 0.0, -jnp.inf)
        return carry

    lax.fori_loop(0, TILES // 2, make_bias, 0)
    yb = row_id(z, oh, c)
    n_y.wait_recv()
    ny_p = nsend(yb, dzp)
    ny_m = nsend(yb, dzm)
    sibs.append(nsend(yb, sib))
    cyp, cym = [], []
    for h in range(HEADS):
        cy[h].wait_recv()
        b = col_id(ol, x)
        cyp.append(qsend(h, b, dxp))
        cym.append(qsend(h, b, dxm))
    lax.fori_loop(TILES // 2, TILES, make_bias, 0)
    project(own)
    project(yb)

    far = []
    for got_p, got_m, h_ in ((n_p, n_m, yh), (ny_p, ny_m, oh)):
        got_p.wait_recv()
        b = row_id(zm, h_, c)
        far.append(nhalf(b, 0, dzp))
        sibs.append(nsend(b, sib))
        project(b)
        got_m.wait_recv()
        b = row_id(zp, h_, c)
        far.append(nhalf(b, 1, dzm))
        sibs.append(nsend(b, sib))
        project(b)

    qfar = []
    for h in range(HEADS):
        for got_p, got_m, l_ in ((cp, cm, yl), (cyp, cym, ol)):
            got_p[h].wait_recv()
            qfar.append(qhalf(h, col_id(l_, xm), 0, dxp))
            got_m[h].wait_recv()
            qfar.append(qhalf(h, col_id(l_, xp), 1, dxm))

    for n, h_ in ((0, yh), (2, oh)):
        b = row_id(zo, h_, c)
        for half in range(2):
            far[n + half].wait_recv()
            sibs.append(nhalf(b, half, sib))
        project(b)
    for d in sibs:
        d.wait_recv()

    def project_other(k, carry):
        project(2 * k + oc)
        return carry

    lax.fori_loop(0, 8, project_other, 0)
    for d in qfar:
        d.wait_recv()

    def forward(h, first, last):
        slot = h % 2

        def step(g, carry):
            for u in range(UNROLL):
                t = g * UNROLL + u
                r, s = meta[0, t], meta[1, t]
                scores = mm_nt(kv[h, s, 0], qd[h][r, 0]) * (SCALE * LOG2E) + bias[t]
                top = jnp.maximum(jnp.max(scores, axis=0, keepdims=True), FLOOR)
                w = jnp.exp2(scores - top)
                dp = mm_nt(kv[h, s, 1], qd[h][r, 1])
                wgt[slot, t] = w
                dpr[slot, t] = dp
                m_s[h, pl.ds(t, 1), :] = top
                l_s[h, pl.ds(t, 1), :] = jnp.sum(w, axis=0, keepdims=True)
                d_s[h, pl.ds(t, 1), :] = jnp.sum(w * dp, axis=0, keepdims=True)
            return carry

        lax.fori_loop(first // UNROLL, last // UNROLL, step, 0)

    def stat_send(h):
        r_of = rcol[...]
        tops, sums, dots = m_s[h], l_s[h], d_s[h]
        for r in range(RB):
            here = r_of == r
            top = jnp.max(jnp.where(here, tops, FLOOR), axis=0, keepdims=True)
            scale = jnp.where(here, jnp.exp2(tops - top), 0.0)
            owner, a = r // 2, r % 2
            st_send[h, owner, a : a + 1, :] = top
            st_send[h, owner, 2 + a : 3 + a, :] = jnp.sum(scale * sums, axis=0, keepdims=True)
            st_send[h, owner, 4 + a : 5 + a, :] = jnp.sum(scale * dots, axis=0, keepdims=True)
        st_recv[h, j] = st_send[h, j]
        return [copy(st_send.at[h, peer[1]], st_recv.at[h, j], peer) for peer in peers]

    def stat_merge(h, sent):
        for d in sent:
            d.wait_recv()
        tops = [st_recv[h, k, 0:2, :] for k in range(8)]
        top = tops[0]
        for k in range(1, 8):
            top = jnp.maximum(top, tops[k])
        total = jnp.zeros((2, 128), F32)
        dot = jnp.zeros((2, 128), F32)
        for k in range(8):
            scale = jnp.exp2(tops[k] - top)
            total = total + scale * st_recv[h, k, 2:4, :]
            dot = dot + scale * st_recv[h, k, 4:6, :]
        gstat[h][j, 0:2, :] = top
        gstat[h][j, 2:4, :] = 1.0 / total
        gstat[h][j, 4:6, :] = dot / total
        return [copy(gstat[h].at[j], gstat[h].at[j], peer) for peer in peers]

    def stat_wait(sent):
        for d in sent:
            d.wait_recv()

    def backward_recv(h):
        slot = h % 2
        acc1[0] = jnp.zeros((TB, HD), F32)
        acc2[0] = jnp.zeros((TB, HD), F32)

        def step(g, carry):
            for u in range(UNROLL):
                t = g * UNROLL + u
                r, s = meta[0, t], meta[1, t]
                owner, a = r // 2, r % 2
                top = gstat[h][owner, pl.ds(a, 1), :]
                inv_total = gstat[h][owner, pl.ds(2 + a, 1), :]
                delta = gstat[h][owner, pl.ds(4 + a, 1), :]
                fix = jnp.exp2(m_s[h, pl.ds(t, 1), :] - top) * inv_total
                prob = wgt[slot, t] * fix
                dscore = prob * (dpr[slot, t] - delta) * SCALE
                prob = prob.astype(BF16)
                dscore = dscore.astype(BF16)
                p_s[t] = prob
                ds_s[t] = dscore
                same = meta[3, t] > 0
                acc1[t + 1] = jnp.where(same, acc1[t], 0.0) + mm_tn(prob, kv[h, s, 1])
                acc2[t + 1] = jnp.where(same, acc2[t], 0.0) + mm_tn(dscore, kv[h, s, 0])
            return carry

        lax.fori_loop(0, TILES // UNROLL, step, 0)
        for r in range(RB):
            at = meta[7, r]
            od[h, r, 0] = acc1[at].astype(BF16)
            od[h, r, 1] = acc2[at].astype(BF16)

    def backward_send(h):
        def step(g, carry):
            for u in range(UNROLL):
                n = g * UNROLL + u
                t, r = meta[5, n], meta[9, n]
                same = meta[6, n] > 0
                acc1[n + 1] = jnp.where(same, acc1[n], 0.0) + mm(ds_s[t], qd[h][r, 0])
                acc2[n + 1] = jnp.where(same, acc2[n], 0.0) + mm(p_s[t], qd[h][r, 1])
            return carry

        lax.fori_loop(0, TILES // UNROLL, step, 0)
        for s in range(SB):
            at = meta[8, s]
            dkv[s, :, h * HD : (h + 1) * HD] = acc1[at].astype(BF16)
            dkv[s, :, D + h * HD : D + (h + 1) * HD] = acc2[at].astype(BF16)

    def osend_a(h):
        sent = []
        for l_ in range(2):
            b = col_id(l_, xo)
            sent.append(copy(od.at[h, 2 * b], ra.at[h, 0, l_], dxp))
            sent.append(copy(od.at[h, 2 * b + 1], ra.at[h, 1, l_], dxm))
        return sent

    def osend_b(h, sent):
        for d in sent:
            d.wait_recv()
        out = []
        for l_ in range(2):
            b = col_id(l_, xp)
            od[h, 2 * b] = (od[h, 2 * b].astype(F32) + ra[h, 0, l_].astype(F32)).astype(BF16)
            out.append(copy(od.at[h, pl.ds(2 * b, 2)], rb.at[h, 0, l_], dxp))
            b = col_id(l_, xm)
            od[h, 2 * b + 1] = (od[h, 2 * b + 1].astype(F32) + ra[h, 1, l_].astype(F32)).astype(BF16)
            out.append(copy(od.at[h, pl.ds(2 * b, 2)], rb.at[h, 1, l_], dxm))
        return out

    def osend_d(h, sent):
        for d in sent:
            d.wait_recv()
        for l_ in (ol, yl):
            b = col_id(l_, x)
            for a in range(2):
                od[h, 2 * b + a] = (
                    od[h, 2 * b + a].astype(F32)
                    + rb[h, 0, l_, a].astype(F32)
                    + rb[h, 1, l_, a].astype(F32)
                ).astype(BF16)
        return copy(od.at[h, pl.ds(2 * col_id(ol, x), 2)], rd.at[h], ylp)

    def ofinish(h, sent):
        sent.wait_recv()
        for a in range(2):
            for k in range(2):
                fin[k, a * TB : (a + 1) * TB, h * HD : (h + 1) * HD] = (
                    od[h, 2 * j + a, k].astype(F32) + rd[h, a, k].astype(F32)
                ).astype(BF16)

    forward(0, 0, TILES)
    s0 = stat_send(0)
    forward(1, 0, TILES // 2)
    g0 = stat_merge(0, s0)
    forward(1, TILES // 2, TILES)
    s1 = stat_send(1)
    stat_wait(g0)
    backward_recv(0)
    a0 = osend_a(0)
    g1 = stat_merge(1, s1)
    backward_send(0)
    b0 = osend_b(0, a0)
    forward(2, 0, TILES)
    s2 = stat_send(2)
    d0 = osend_d(0, b0)
    stat_wait(g1)
    backward_recv(1)
    a1 = osend_a(1)
    g2 = stat_merge(2, s2)
    backward_send(1)
    b1 = osend_b(1, a1)
    ofinish(0, d0)
    forward(3, 0, TILES)
    s3 = stat_send(3)
    d1 = osend_d(1, b1)
    stat_wait(g2)
    backward_recv(2)
    a2 = osend_a(2)
    g3 = stat_merge(3, s3)
    backward_send(2)
    b2 = osend_b(2, a2)
    ofinish(1, d1)
    stat_wait(g3)
    backward_recv(3)
    a3 = osend_a(3)
    d2 = osend_d(2, b2)
    backward_send(3)
    b3 = osend_b(3, a3)

    for d in [n_y, n_p, n_m, ny_p, ny_m] + sibs + far:
        d.wait_send()

    def pair_back(b):
        pair = dkv[pl.ds(2 * b, 2)].reshape(OWN, 2 * D)
        nall[b] = (mm_nt(pair[:, :D], wk[...]) + mm_nt(pair[:, D:], wv[...])).astype(BF16)

    tosib = []
    for n, z_ in enumerate((zo, zp, zm, z)):
        for h_ in range(2):
            b = row_id(z_, h_, oc)
            pair_back(b)
            tosib.append(copy(nall.at[b], pd.at[n, h_], sib))
    for z_ in (zo, zp, zm, z):
        for h_ in range(2):
            pair_back(row_id(z_, h_, c))
    d3 = osend_d(3, b3)
    ofinish(2, d2)

    def merge_sib(n, z_, h_):
        tosib[2 * n + h_].wait_recv()
        b = row_id(z_, h_, c)
        nall[b] = (nall[b].astype(F32) + pd[n, h_].astype(F32)).astype(BF16)

    pa_sent = []
    for h_ in range(2):
        merge_sib(0, zo, h_)
        b = row_id(zo, h_, c)
        pa_sent.append(copy(nall.at[b, pl.ds(0, TB)], pa.at[0, h_], dzp))
        pa_sent.append(copy(nall.at[b, pl.ds(TB, TB)], pa.at[1, h_], dzm))
    for h_ in range(2):
        merge_sib(1, zp, h_)
        merge_sib(2, zm, h_)
        merge_sib(3, z, h_)
    pb_sent = []
    for h_ in range(2):
        for side, z_, dev in ((0, zp, dzp), (1, zm, dzm)):
            pa_sent[2 * h_ + side].wait_recv()
            b = row_id(z_, h_, c)
            part = slice(side * TB, (side + 1) * TB)
            nall[b, part, :] = (
                nall[b, part, :].astype(F32) + pa[side, h_].astype(F32)
            ).astype(BF16)
            pb_sent.append(copy(nall.at[b], pb.at[side, h_], dev))
    ofinish(3, d3)

    update = mm(fin[0], wo[...]).astype(BF16)
    out_update[...] = mm_tn(perm_s[...], update).astype(BF16)
    d_normed = mm_nt(fin[1], wq[...])

    for d in pb_sent:
        d.wait_recv()

    def z_sum(h_):
        return (
            nall[row_id(z, h_, c)].astype(F32)
            + pb[0, h_].astype(F32)
            + pb[1, h_].astype(F32)
        )

    nall[row_id(z, oh, c)] = z_sum(oh).astype(BF16)
    pe_sent = copy(nall.at[row_id(z, oh, c)], pe, yhp)
    d_normed = d_normed + z_sum(yh)
    pe_sent.wait_recv()
    d_normed = d_normed + pe[...].astype(F32)
    scaled = d_normed * gain[...]
    unit = unit_s[...]
    grad = inv_s[:, 0:1] * (
        scaled
        - jnp.mean(scaled, axis=1, keepdims=True)
        - unit * jnp.mean(scaled * unit, axis=1, keepdims=True)
    )
    out_grad[...] = mm_tn(perm_s[...], grad.astype(BF16)).astype(BF16)

    waited = [n_y, n_p, n_m, ny_p, ny_m] + sibs + far
    for d in made:
        if not any(d is w for w in waited):
            d.wait_send()


def order_lists(tile_index, tile_count):
    slots = jnp.arange(TILES, dtype=jnp.int32)
    live = slots < tile_count
    r = jnp.clip(tile_index[:, 0], 0, RB - 1)
    s = jnp.clip(tile_index[:, 1], 0, SB - 1)

    def sort_places(key):
        whole = key * TILES + slots
        rank = jnp.sum((whole[:, None] > whole[None, :]).astype(jnp.int32), axis=1)
        return (rank[None, :] == slots[:, None]).astype(jnp.int32)

    def take(pick, values):
        return jnp.sum(pick * values[None, :], axis=1)

    def same_as_before(key):
        return jnp.concatenate([jnp.zeros((1,), jnp.int32), (key[1:] == key[:-1]).astype(jnp.int32)])

    def last_of(key, count):
        blocks = jnp.arange(TILES, dtype=jnp.int32)
        hit = key[None, :] == blocks[:, None]
        return jnp.max(jnp.where(hit, slots[None, :] + 1, 0), axis=1)

    by_r = sort_places(r)
    r1, s1 = take(by_r, r), take(by_r, s)
    slot1 = take(by_r, slots)
    limit = jnp.where(take(by_r, live.astype(jnp.int32)) > 0, 0, 2)
    by_s = sort_places(s1)
    place2 = take(by_s, slots)
    r2, s2 = take(by_s, r1), take(by_s, s1)
    meta = jnp.stack(
        [
            r1,
            s1,
            slot1,
            same_as_before(r1),
            limit,
            place2,
            same_as_before(s2),
            last_of(r1, RB),
            last_of(s2, SB),
            r2,
        ]
    )
    return meta, jnp.broadcast_to(r1[:, None], (TILES, 128))


def local(
    nodes,
    gain,
    w_query,
    w_key,
    w_value,
    w_out,
    cotangent,
    tile_index,
    tile_mask,
    tile_count,
    node_order,
):
    meta, rcol = order_lists(tile_index[0, 0], tile_count[0, 0])
    order = (node_order % OWN).reshape(1, OWN)
    vmem = pl.BlockSpec(memory_space=pltpu.VMEM)
    smem = pl.BlockSpec(memory_space=pltpu.SMEM)
    out = jax.ShapeDtypeStruct((OWN, D), BF16)
    return pl.pallas_call(
        body,
        out_shape=(out, out),
        in_specs=[smem] + [vmem] * 10,
        out_specs=(vmem, vmem),
        scratch_shapes=[
            pltpu.VMEM((OWN, OWN), BF16),
            pltpu.VMEM((OWN, D), F32),
            pltpu.VMEM((OWN, 128), F32),
            pltpu.VMEM((16, OWN, D), BF16),
            *[pltpu.VMEM((RB, 2, TB, HD), BF16)] * HEADS,
            pltpu.VMEM((HEADS, SB, 2, TB, HD), BF16),
            pltpu.VMEM((TILES, TB, TB), F32),
            pltpu.VMEM((2, TILES, TB, TB), F32),
            pltpu.VMEM((2, TILES, TB, TB), F32),
            pltpu.VMEM((HEADS, TILES, 128), F32),
            pltpu.VMEM((HEADS, TILES, 128), F32),
            pltpu.VMEM((HEADS, TILES, 128), F32),
            pltpu.VMEM((TILES, TB, TB), BF16),
            pltpu.VMEM((TILES, TB, TB), BF16),
            pltpu.VMEM((TILES + 1, TB, HD), F32),
            pltpu.VMEM((TILES + 1, TB, HD), F32),
            pltpu.VMEM((HEADS, RB, 2, TB, HD), BF16),
            pltpu.VMEM((HEADS, 2, 2, 2, TB, HD), BF16),
            pltpu.VMEM((HEADS, 2, 2, 2, 2, TB, HD), BF16),
            pltpu.VMEM((HEADS, 2, 2, TB, HD), BF16),
            pltpu.VMEM((2, OWN, D), BF16),
            pltpu.VMEM((SB, TB, 2 * D), BF16),
            pltpu.VMEM((4, 2, OWN, D), BF16),
            pltpu.VMEM((2, 2, TB, D), BF16),
            pltpu.VMEM((2, 2, OWN, D), BF16),
            pltpu.VMEM((OWN, D), BF16),
            pltpu.VMEM((HEADS, 8, 8, 128), F32),
            pltpu.VMEM((HEADS, 8, 8, 128), F32),
            *[pltpu.VMEM((8, 8, 128), F32)] * HEADS,
            pltpu.SemaphoreType.DMA((SEMS,)),
            pltpu.SemaphoreType.DMA((SEMS,)),
        ],
        compiler_params=pltpu.CompilerParams(
            collective_id=0,
            has_side_effects=True,
            vmem_limit_bytes=63 * 1024 * 1024,
        ),
        cost_estimate=pl.CostEstimate(
            flops=13_000_000_000, bytes_accessed=8_000_000, transcendentals=2_100_000
        ),
    )(
        meta,
        order,
        rcol,
        nodes,
        cotangent,
        gain.reshape(1, D),
        w_query,
        w_key,
        w_value,
        w_out,
        tile_mask[0, 0],
    )


def solution(mesh):
    placed = (
        P(("row", "col"), None),
        P(),
        P(),
        P(),
        P(),
        P(),
        P(("row", "col"), None),
        P("row", "col", None, None),
        P("row", "col", None, None, None),
        P("row", "col"),
        P(("row", "col")),
    )
    return jax.shard_map(
        local,
        mesh=mesh,
        in_specs=placed,
        out_specs=(P(("row", "col"), None), P(("row", "col"), None)),
        check_vma=False,
    )
```

time: 860 us -> 150 us (0.17); the launches traced: 850 us -> 150 us
  waiting for transfers between devices: 310 us -> 0 us
  local copies, waits for them, and re-layouts: 286 us -> 5.24 us
  Pallas kernels: 0 us -> 139 us
  other arithmetic: 109 us -> 3.74 us
  blocking collectives: 64.4 us -> 0 us
  matrix products: 62.8 us -> 0 us
  between operations: 15.3 us -> 1.33 us
    reduce_scatter x3 -> x0, waiting for transfers between devices: 160 us -> none  [the longest x1 82.7 us: local(): lax.psum_scatter(value_flat.astype(jnp.bfloat16), 'row', scatter_dimensio...]
    pallas_call x0 -> x1, Pallas kernels: none -> 139 us  [local(): pl.pallas_call(body, out_shape=(out, out), in_specs=[smem] + [vmem] * 10,...]
    gather x54 -> x0, local copies, waits for them, and re-layouts: 134 us -> none  [the longest x12 57.6 us: group_tiles(): pair_tile = pair_blocks[send_idx]]
    all_gather x3 -> x0, waiting for transfers between devices: 107 us -> none  [the longest x1 71.1 us: local(): pair_rows = lax.all_gather(own_pair, 'row', axis=0, tiled=True)]
    scatter-add x20 -> x0, other arithmetic: 74.6 us -> none  [the longest x4 20.3 us: grad_step(): key_acc.at[send_idx]]
    dot_general x39 -> x0, matrix products: 62.8 us -> none  [the longest x12 17 us: group_scores(): jnp.einsum('gahd,gbhd->ghab', query_tile, key_tile, preferred_element_typ...]
    psum x1 -> x0, waiting for transfers between devices: 43.2 us -> none  [local(): lax.psum(weighted.astype(jnp.bfloat16), 'col').astype(jnp.float32)]
    transpose x16 -> x0, local copies, waits for them, and re-layouts: 39.2 us -> none  [the longest x4 12.1 us: grad_step(): jnp.einsum('ghab,gahd->gbhd', norm_weight.astype(jnp.bfloat16), grad_tile...]
  transfers between devices with their start and end apart: 7 -> 0, of which waited for: 5 -> 0; matrix products, arithmetic and copies ran while one was open for 24% -> 0% of each run, Pallas kernels for 0% -> 0%
where the time goes in v1:
time: 150 us
  Pallas kernels  139 us (93%)
  local copies, waits for them, and re-layouts  5.24 us (3%)
  other arithmetic  3.74 us (2%)
    pallas_call x1, Pallas kernels, local(): pl.pallas_call(body, out_shape=(out, out), in_specs=[smem] + [vmem] * 10,...  139 us
    unnamed x2, local copies, waits for them, and re-layouts  3.34 us

profile of v1, /device:TPU:0, one launch (start us, length us, event | category | flops | bytes accessed | tf_op | source)
XLA Modules:
  0.0 149.5 jit_solution(11017448407718081017)
XLA Ops:
  1.3 0.7 iota_add_fusion.2
  2.0 1.3 and_select_fusion
  3.3 0.8 fusion.6
  4.0 0.2 convert_reduce_fusion.1
  4.2 0.2 select_reduce_fusion.5
  4.4 0.2 convert_reduce_fusion
  4.6 0.1 slice_compare_fusion.1
  4.6 0.2 select_reduce_fusion
  4.8 0.1 select_reduce_fusion.1
  4.9 0.1 slice_compare_fusion
  5.0 0.1 fusion.4
  5.1 1.2 stack.48.meta
  6.3 0.7 broadcast_in_dim.22.rcol
  7.0 139.2 %shard_map.122 = (bf16[256,512]{1,0:T(8,128)(2,1)}, bf16[256,512]{1,0:T(8,128)(2,1)}) custom-call(s32[10,32]{1,0:T(8,128)} %stack.48.meta, s32[1,256]{1,0:T(1,128)} %bitcast.35, s32[32,128]{1,0:T(8,128)} %broadcast_in_dim.22.rcol, bf16[256,512]{1,0:T(8,128)(2,1)} %nodes.1, bf16[256,512]{1,0:T(8,128)(2,1)} %cot.1, f32[1,512]{1,0:T(1,128)} %bitcast.38, ...), custom_call_target="tpu_custom_call" | custom-call | flops 12999999488 | bytes 8000000 | tf_op jit(solution)/shard_map/pallas_call | solution.py:581
  146.2 1.7 %copy.16 = bf16[256,512]{1,0:T(8,128)(2,1)} copy(bf16[256,512]{1,0:T(8,128)(2,1)} %get-tuple-element.17) | data formatting | bytes 524288
  147.8 1.7 %copy.17 = bf16[256,512]{1,0:T(8,128)(2,1)} copy(bf16[256,512]{1,0:T(8,128)(2,1)} %get-tuple-element.18) | data formatting | bytes 524288
  (4 shorter events, 0.0 us)
